TPU v7x, 32 devices: a whole 2x2x4 slice. The times are simulated.
32 devices in a mesh: rep: 4 (over y, x), shard: 8 (over z, core).
Axes of the slice: x: 2, y: 2, z: 4, core: 2. Of those that a mesh axis runs over, the one named last changes fastest.
Arguments:
- bag_ids: int32 [2048, 20], P(('rep', 'shard')), may hold values from 0 to 4095
- table: float32 [4096, 256], P('shard'), may hold values from -1.2 to 1.2
- accum: float32 [4096], P('shard'), may hold values from 0.01 to 0.1
- cross_weight: float32 [256, 256], replicated, may hold values from -0.375 to 0.375
- cross_bias: float32 [256], replicated, may hold values from -4 to 4
- upstream: float32 [2048, 256], P(('rep', 'shard')), may hold values from -6 to 6
Outputs:
- crossed: float32 [2048, 256], P(('rep', 'shard'))
- new_table: float32 [4096, 256], P('shard')
- new_accum: float32 [4096], P('shard')
All inputs are finite; a program needn't handle non-finite values.
Results may differ from a plain program's by a relative error of at most 0.00014.
Values sent between devices are 32-bit elements; how exact they have to be, the bound alone decides.
A program may use at most 64 MiB of HBM per device.

v0:
```python
import jax
import jax.numpy as jnp
from jax import lax
from jax.experimental import pallas as pl
from jax.experimental.pallas import tpu as pltpu
from jax.sharding import PartitionSpec as P

F32 = jnp.float32
BF16 = jnp.bfloat16
MESH = pl.DeviceIdType.MESH
PLANE = 4
LINE = 4
GRANT = 63 * 1024 * 1024
CHUNK = 256


def split(x):
    hi = x.astype(BF16)
    return hi, (x - hi.astype(F32)).astype(BF16)


def dot(a, b, dims=((1,), (0,))):
    return lax.dot_general(a, b, (dims, ((), ())), preferred_element_type=F32)


def kernel(
    bag, ids_hbm, table_hbm, accum_hbm, weight_hbm, bias_hbm, up_hbm,
    crossed_out, newt_out, newa_out,
    tab, thi, tlo, ids, ct, psend, precv, back, g, grecv,
    ids_raw, accum, weight, bias, up, wsp, crossed_ref, newt_ref, newa_ref,
    load_sem, store_sem, tab_sem, idz_sem, idp_sem, p_sem, bz_sem, bp_sem, bd_sem, g_sem,
):
    rep = lax.axis_index("rep")
    shard = lax.axis_index("shard")
    z = shard // 2
    core = shard % 2
    rows = tab.shape[1]
    each = up.shape[0]
    mate = (rep, shard + 1 - 2 * core)
    xn = (rep + 1 - 2 * (rep % 2), shard)
    yn = ((rep + 2) % 4, shard)
    line = {
        1: (rep, (z + 1 - 2 * (z % 2)) * 2 + core),
        2: (rep, ((z + 2) % LINE) * 2 + core),
        3: (rep, (LINE - 1 - z) * 2 + core),
    }

    def send(src, dst, sems, to):
        cp = pltpu.make_async_remote_copy(
            src_ref=src, dst_ref=dst, send_sem=sems.at[0], recv_sem=sems.at[1],
            device_id=to, device_id_type=MESH,
        )
        cp.start()
        return cp

    barrier = pltpu.get_barrier_semaphore()
    for to in (mate, xn, yn, line[1], line[2], line[3]):
        pl.semaphore_signal(barrier, inc=1, device_id=to, device_id_type=MESH)

    def load(src, dst, i):
        cp = pltpu.make_async_copy(src, dst, load_sem.at[i])
        cp.start()
        return cp

    ids_load = load(ids_hbm, ids_raw, 0)
    table_load = load(table_hbm, tab.at[0], 1)
    rest = [
        load(src, dst, 2 + i)
        for i, (src, dst) in enumerate(
            ((weight_hbm, weight), (up_hbm, up), (bias_hbm, bias), (accum_hbm, accum))
        )
    ]
    ids_load.wait()
    raw = ids_raw[...]
    ids[0, 0] = jnp.full(ids.shape[2:], -1, jnp.int32)
    ids[0, 0, 0:bag] = jnp.concatenate([raw, raw], axis=1)
    pl.semaphore_wait(barrier, 6)

    idz = {j: send(ids.at[0, 0], ids.at[0, j], idz_sem.at[j - 1], line[j]) for j in (2, 3, 1)}
    tcp = send(table_hbm, tab.at[1], tab_sem, mate)
    table_load.wait()
    hi, lo = split(tab[0])
    thi[0:rows] = hi
    tlo[0:rows] = lo

    for cp in rest:
        cp.wait()
    hi, lo = split(weight[...])
    wsp[0] = hi
    wsp[1] = lo
    turned = jnp.transpose(weight[...])
    hi, lo = split(turned)
    wsp[2] = hi
    wsp[3] = lo

    own_first = shard * rows
    mate_first = (shard + 1 - 2 * core) * rows
    per_block = rows // CHUNK
    row16 = lax.broadcasted_iota(jnp.int32, (CHUNK, 128), 0).astype(F32).astype(BF16)
    lane = lax.broadcasted_iota(jnp.int32, ids.shape[2:], 1)
    spot = lax.broadcasted_iota(jnp.int32, ids.shape[2:], 0)
    half = each // 2

    def count(r, p):
        pair = jnp.where(lane < each, ids[r, 2 * p], ids[r, 2 * p + 1])
        times = jnp.ones(pair.shape, F32)
        for i in range(bag - 1):
            again = (spot > i) & (pair == pair[i : i + 1])
            times = times + jnp.where(again, 1.0, 0.0)

        def widen(row):
            one = jnp.broadcast_to(row, (16, 128)).astype(BF16)
            return jnp.concatenate([one] * (CHUNK // 16), axis=0)

        def step(q, carry):
            base = jnp.where(q < per_block, own_first, mate_first) + (q % per_block) * CHUNK
            local = pair - base
            local = jnp.where((local >= 0) & (local < CHUNK), local, -1).astype(F32)
            acc = jnp.zeros((CHUNK, 128), BF16)
            for j in range(bag):
                acc = jnp.where(widen(local[j : j + 1]) == row16, widen(times[j : j + 1]), acc)
            ct[r, pl.ds(pl.multiple_of(q * CHUNK, CHUNK), CHUNK), pl.ds(p * 128, 128)] = acc
            return carry

        lax.fori_loop(0, 2 * per_block, step, 0)

    pcp = {}
    mine = None

    def give(j, h):
        part = pl.ds(h * half, half)
        pcp[j, h] = send(psend.at[j - 1, part], precv.at[j - 1, part], p_sem.at[j - 1, h], line[j])

    for p in (1, 0):
        for j in ((2, 3) if p else (1,)):
            idz[j].wait()
        if not p:
            idx = send(ids.at[0], ids.at[1], idp_sem.at[0], xn)
            idy = send(ids.at[0], ids.at[2], idp_sem.at[1], yn)
        count(0, p)
        if p:
            tcp.wait()
            hi, lo = split(tab[1])
            thi[rows : 2 * rows] = hi
            tlo[rows : 2 * rows] = lo
        c = ct[0, :, p * 128 : (p + 1) * 128]
        part = dot(c, thi[...], ((0,), (0,))) + dot(c, tlo[...], ((0,), (0,)))
        for i in (0, 1):
            j = 2 * p + i
            piece = part[i * each : (i + 1) * each]
            if j == 0:
                mine = piece
            else:
                psend[j - 1] = piece
                give(j, 0)
    for j in (2, 3, 1):
        give(j, 1)

    idx.wait()
    idd = send(ids.at[1], ids.at[3], idp_sem.at[2], yn)
    count(1, 0)
    count(1, 1)

    def cross(x, k):
        xh, xl = split(x)
        return dot(xh, wsp[k]) + (dot(xh, wsp[k + 1]) + dot(xl, wsp[k]))

    def block(r, j, h):
        return back.at[r, pl.ds(j * each + h * half, half)]

    zcp, xcp, ycp, dcp = {}, {}, {}, {}

    def forward(j, h):
        xcp[j, h] = send(block(0, j, h), block(1, j, h), bp_sem.at[0, j, h], xn)
        ycp[j, h] = send(block(0, j, h), block(2, j, h), bp_sem.at[1, j, h], yn)

    def process(h):
        at = slice(h * half, (h + 1) * half)
        for j in (1, 2, 3):
            pcp[j, h].wait()
        pooled = (mine[at] + precv[0, at]) + (precv[1, at] + precv[2, at])
        grad = up[at]
        mixed = cross(pooled, 0) + bias[...]
        back[0, at] = grad * mixed + cross(grad * pooled, 2) + grad
        for j in (2, 1):
            zcp[j, h] = send(block(0, 0, h), block(0, j, h), bz_sem.at[j - 1, h], line[j])
        forward(0, h)
        crossed_ref[at] = pooled * mixed + pooled

    def along(j, h):
        zcp[j, h].wait_recv()
        if j == 2:
            zcp[3, h] = send(block(0, 2, h), block(0, 3, h), bz_sem.at[2, h], line[1])
        forward(j, h)

    def diagonal(j, h):
        xcp[j, h].wait_recv()
        ycp[j, h].wait_recv()
        if (j + h) % 2:
            dcp[j, h] = send(block(1, j, h), block(3, j, h), bd_sem.at[j, h], yn)
        else:
            dcp[j, h] = send(block(2, j, h), block(3, j, h), bd_sem.at[j, h], xn)

    process(0)
    idy.wait()
    count(2, 0)
    process(1)
    stores = [pltpu.make_async_copy(crossed_ref, crossed_out, store_sem.at[0])]
    stores[0].start()
    along(1, 0)
    along(2, 0)
    diagonal(0, 0)
    count(2, 1)
    along(3, 0)
    along(1, 1)
    diagonal(1, 0)
    along(2, 1)
    diagonal(0, 1)
    idd.wait()
    count(3, 0)
    diagonal(2, 0)
    along(3, 1)
    diagonal(1, 1)
    diagonal(3, 0)
    count(3, 1)
    diagonal(2, 1)
    diagonal(3, 1)

    def product(r, start=0, size=2 * rows):
        bh, bl = split(back[r])
        c = ct[r, start : start + size]
        g[r, start : start + size] = dot(c, bh) + dot(c, bl)

    product(0)
    product(1)
    product(2)
    for cp in dcp.values():
        cp.wait_recv()

    def finish(start, size):
        product(3, start, size)
        at = slice(start, start + size)
        g[0, at] = (g[0, at] + g[1, at]) + (g[2, at] + g[3, at])

    piece = rows // 2
    gcp = []
    for i in range(2):
        finish(rows + i * piece, piece)
        gcp.append(
            send(g.at[0, pl.ds(rows + i * piece, piece)], grecv.at[pl.ds(i * piece, piece)], g_sem.at[i], mate)
        )
    finish(0, rows)
    acc_col = jnp.transpose(jnp.broadcast_to(accum[...], (8, rows)))[:, 0:1]
    for d in (zcp, xcp, ycp, dcp):
        for cp in d.values():
            cp.wait_send()
    for i in range(2):
        gcp[i].wait()
        at = slice(i * piece, (i + 1) * piece)
        total = g[0, at] + grecv[at]
        mean = jnp.sum(total * total, axis=1, keepdims=True) * (1.0 / total.shape[1])
        fresh = acc_col[at] + mean
        newt_ref[at] = tab[0, at] - 0.5 * total * lax.rsqrt(fresh)
        part = pl.ds(i * piece, piece)
        stores.append(pltpu.make_async_copy(newt_ref.at[part], newt_out.at[part], store_sem.at[1 + i]))
        stores[-1].start()
        newa_ref[:, at] = jnp.transpose(jnp.broadcast_to(fresh, (piece, 128)))[0:1]
    stores.append(pltpu.make_async_copy(newa_ref, newa_out, store_sem.at[3]))
    stores[-1].start()
    for cp in stores:
        cp.wait()


def hand_out(a, b, c, x, y, w, va, vb, vc, sems_in, sems_out):
    piece = vb.shape[0] // 2
    parts = [(b.at[pl.ds(i * piece, piece)], vb.at[pl.ds(i * piece, piece)], y.at[pl.ds(i * piece, piece)]) for i in (0, 1)]
    parts += [(a, va, x), (c, vc, w)]
    ins = [pltpu.make_async_copy(p[0], p[1], sems_in.at[i]) for i, p in enumerate(parts)]
    outs = [pltpu.make_async_copy(p[1], p[2], sems_out.at[i]) for i, p in enumerate(parts)]
    for cp in ins:
        cp.start()
    for cp, out in zip(ins, outs):
        cp.wait()
        out.start()
    for cp in outs:
        cp.wait()


def fused_body(bag_ids, table, accum, cross_weight, cross_bias, upstream):
    each, bag = bag_ids.shape
    rows, width = table.shape
    tall = -(-bag // 8) * 8
    hbm = pl.BlockSpec(memory_space=pltpu.HBM)
    dma = pltpu.SemaphoreType.DMA
    shapes = (
        jax.ShapeDtypeStruct((each, width), F32),
        jax.ShapeDtypeStruct((rows, width), F32),
        jax.ShapeDtypeStruct((1, rows), F32),
    )
    done = pl.pallas_call(
        lambda *refs: kernel(bag, *refs),
        out_shape=shapes,
        in_specs=[hbm] * 6,
        out_specs=[hbm] * 3,
        scratch_shapes=[
            pltpu.VMEM((2, rows, width), F32),
            pltpu.VMEM((2 * rows, width), BF16),
            pltpu.VMEM((2 * rows, width), BF16),
            pltpu.VMEM((PLANE, LINE, tall, 128), jnp.int32),
            pltpu.VMEM((PLANE, 2 * rows, LINE * each), BF16),
            pltpu.VMEM((LINE - 1, each, width), F32),
            pltpu.VMEM((LINE - 1, each, width), F32),
            pltpu.VMEM((PLANE, LINE * each, width), F32),
            pltpu.VMEM((PLANE, 2 * rows, width), F32),
            pltpu.VMEM((rows, width), F32),
            pltpu.VMEM((bag, each), jnp.int32),
            pltpu.VMEM((1, rows), F32),
            pltpu.VMEM((width, width), F32),
            pltpu.VMEM((1, width), F32),
            pltpu.VMEM((each, width), F32),
            pltpu.VMEM((4, width, width), BF16),
            pltpu.VMEM((each, width), F32),
            pltpu.VMEM((rows, width), F32),
            pltpu.VMEM((1, rows), F32),
            dma((6,)),
            dma((4,)),
            dma((2,)),
            dma((3, 2)),
            dma((3, 2)),
            dma((3, 2, 2)),
            dma((3, 2, 2)),
            dma((2, LINE, 2, 2)),
            dma((LINE, 2, 2)),
            dma((2, 2)),
        ],
        compiler_params=pltpu.CompilerParams(
            collective_id=0, has_side_effects=True, vmem_limit_bytes=GRANT
        ),
    )(bag_ids.T, table, accum.reshape(1, rows), cross_weight, cross_bias.reshape(1, width), upstream)
    crossed, new_table, new_accum = pl.pallas_call(
        hand_out,
        out_shape=shapes,
        in_specs=[hbm] * 3,
        out_specs=[hbm] * 3,
        scratch_shapes=[pltpu.VMEM(a.shape, F32) for a in shapes] + [dma((4,)), dma((4,))],
        compiler_params=pltpu.CompilerParams(vmem_limit_bytes=GRANT),
    )(*done)
    return crossed, new_table, new_accum.reshape(rows)


def adagrad_rows(rows, sums, grads):
    fresh = sums + jnp.mean(grads * grads, axis=1)
    return (rows - 0.5 * grads / jnp.sqrt(fresh)[:, None], fresh)


def general_body(bag_ids, table, accum, cross_weight, cross_bias, upstream):
    rows_owned = table.shape[0]
    first_row = lax.axis_index("shard") * rows_owned
    group_ids = lax.all_gather(bag_ids, "shard", axis=0, tiled=True)
    local = group_ids - first_row
    number = lax.broadcasted_iota(jnp.int32, (1, rows_owned), 1)
    counts = jnp.zeros((local.shape[0], rows_owned), F32)
    for j in range(local.shape[1]):
        counts = counts + (local[:, j : j + 1] == number).astype(F32)
    pooled = lax.psum_scatter(
        jnp.dot(counts, table, precision=lax.Precision.HIGHEST),
        "shard",
        scatter_dimension=0,
        tiled=True,
    )
    mixed = jnp.dot(pooled, cross_weight, precision=lax.Precision.HIGHEST) + cross_bias
    crossed = pooled * mixed + pooled
    back = (
        upstream * mixed
        + jnp.dot(upstream * pooled, cross_weight.T, precision=lax.Precision.HIGHEST)
        + upstream
    )
    piece = lax.all_gather(back, "shard", axis=0, tiled=True)
    added = lax.dot_general(
        counts, piece, (((0,), (0,)), ((), ())), precision=lax.Precision.HIGHEST
    )
    totals = lax.psum(added, "rep")
    new_table, new_accum = adagrad_rows(table, accum, totals)
    return (crossed, new_table, new_accum)


def solution(mesh):
    placed = (
        P(("rep", "shard"), None),
        P("shard", None),
        P("shard"),
        P(),
        P(),
        P(("rep", "shard"), None),
    )
    small = mesh.shape["rep"] == PLANE and mesh.shape["shard"] == 2 * LINE
    return jax.shard_map(
        fused_body if small else general_body,
        mesh=mesh,
        in_specs=placed,
        out_specs=(P(("rep", "shard"), None), P("shard", None), P("shard")),
        check_vma=False,
    )
```

profile of v0, /device:TPU:0, one launch (start us, length us, event | category | flops | bytes accessed | tf_op | source)
XLA Modules:
  0.0 37.4 jit_solution(298877284699632064)
XLA Ops:
  0.6 34.9 %shard_map.85 = (f32[64,256]{1,0:T(8,128)}, f32[512,256]{1,0:T(8,128)}, f32[1,512]{1,0:T(1,128)}) custom-call(s32[20,64]{1,0:T(8,128)} %bitcast.4, f32[512,256]{1,0:T(8,128)} %refs_1_.1, f32[1,512]{1,0:T(1,128)} %bitcast.5, f32[256,256]{1,0:T(8,128)} %refs_3_.1, f32[1,256]{1,0:T(1,128)} %bitcast.6, f32[64,256]{1,0:T(8,128)} %refs_5_.1), custom_call_target="tpu_custom_call" | custom-call | tf_op jit(solution)/shard_map/pallas_call | solution.py:300
  35.6 1.8 %shard_map.86 = (f32[64,256]{1,0:T(8,128)}, f32[512,256]{1,0:T(8,128)}, f32[1,512]{1,0:T(1,128)}) custom-call(f32[64,256]{1,0:T(8,128)} %get-tuple-element.9.a, f32[512,256]{1,0:T(8,128)} %get-tuple-element.10.b, f32[1,512]{1,0:T(1,128)} %get-tuple-element.11.c), custom_call_target="tpu_custom_call" | custom-call | tf_op jit(solution)/shard_map/pallas_call | solution.py:340
where the time goes:
time: 37.6 us; the launch traced here: 37.4 us
  Pallas kernels  36.7 us (98%)
  between operations  0.64 us (2%)
    pallas_call x1, Pallas kernels, fused_body(): pl.pallas_call(lambda *refs: kernel(bag, *refs), out_shape=shapes, in_spe...  34.9 us
    pallas_call x1, Pallas kernels, fused_body(): pl.pallas_call(hand_out, out_shape=shapes, in_specs=[hbm] * 3, out_specs=...  1.82 us

commit v1 on v0

--- a/solution.py
+++ b/solution.py
@@ -101,16 +101,16 @@
     spot = lax.broadcasted_iota(jnp.int32, ids.shape[2:], 0)
     half = each // 2
 
-    def count(r, p):
+    def widen(row):
+        one = jnp.broadcast_to(row, (16, 128)).astype(BF16)
+        return jnp.concatenate([one] * (CHUNK // 16), axis=0)
+
+    def count(r, p, use=None, start=0):
         pair = jnp.where(lane < each, ids[r, 2 * p], ids[r, 2 * p + 1])
         times = jnp.ones(pair.shape, F32)
         for i in range(bag - 1):
             again = (spot > i) & (pair == pair[i : i + 1])
             times = times + jnp.where(again, 1.0, 0.0)
-
-        def widen(row):
-            one = jnp.broadcast_to(row, (16, 128)).astype(BF16)
-            return jnp.concatenate([one] * (CHUNK // 16), axis=0)
 
         def step(q, carry):
             base = jnp.where(q < per_block, own_first, mate_first) + (q % per_block) * CHUNK
@@ -119,47 +119,51 @@
             acc = jnp.zeros((CHUNK, 128), BF16)
             for j in range(bag):
                 acc = jnp.where(widen(local[j : j + 1]) == row16, widen(times[j : j + 1]), acc)
-            ct[r, pl.ds(pl.multiple_of(q * CHUNK, CHUNK), CHUNK), pl.ds(p * 128, 128)] = acc
+            at = pl.ds(pl.multiple_of(q * CHUNK, CHUNK), CHUNK)
+            ct[r, p, at] = acc
+            return carry if use is None else use(acc, at, carry)
+
+        return lax.fori_loop(0, 2 * per_block, step, start)
+
+    def counts(r):
+        def step(p, carry):
+            count(r, p)
             return carry
 
-        lax.fori_loop(0, 2 * per_block, step, 0)
+        lax.fori_loop(0, 2, step, 0)
 
     pcp = {}
-    mine = None
 
     def give(j, h):
         part = pl.ds(h * half, half)
-        pcp[j, h] = send(psend.at[j - 1, part], precv.at[j - 1, part], p_sem.at[j - 1, h], line[j])
+        pcp[j, h] = send(psend.at[j, part], precv.at[j - 1, part], p_sem.at[j - 1, h], line[j])
+
+    def add_part(acc, at, total):
+        return total + dot(acc, thi[at], ((0,), (0,))) + dot(acc, tlo[at], ((0,), (0,)))
 
     for p in (1, 0):
         for j in ((2, 3) if p else (1,)):
             idz[j].wait()
-        if not p:
-            idx = send(ids.at[0], ids.at[1], idp_sem.at[0], xn)
-            idy = send(ids.at[0], ids.at[2], idp_sem.at[1], yn)
-        count(0, p)
         if p:
             tcp.wait()
             hi, lo = split(tab[1])
             thi[rows : 2 * rows] = hi
             tlo[rows : 2 * rows] = lo
-        c = ct[0, :, p * 128 : (p + 1) * 128]
-        part = dot(c, thi[...], ((0,), (0,))) + dot(c, tlo[...], ((0,), (0,)))
-        for i in (0, 1):
-            j = 2 * p + i
-            piece = part[i * each : (i + 1) * each]
-            if j == 0:
-                mine = piece
-            else:
-                psend[j - 1] = piece
+        else:
+            idx = send(ids.at[0], ids.at[1], idp_sem.at[0], xn)
+            idy = send(ids.at[0], ids.at[2], idp_sem.at[1], yn)
+        part = count(0, p, add_part, jnp.zeros((128, tab.shape[2]), F32))
+        psend[2 * p] = part[0:each]
+        psend[2 * p + 1] = part[each : 2 * each]
+        for j in (2 * p, 2 * p + 1):
+            if j:
                 give(j, 0)
     for j in (2, 3, 1):
         give(j, 1)
 
     idx.wait()
     idd = send(ids.at[1], ids.at[3], idp_sem.at[2], yn)
-    count(1, 0)
-    count(1, 1)
+    counts(1)
 
     def cross(x, k):
         xh, xl = split(x)
@@ -178,18 +182,18 @@
         at = slice(h * half, (h + 1) * half)
         for j in (1, 2, 3):
             pcp[j, h].wait()
-        pooled = (mine[at] + precv[0, at]) + (precv[1, at] + precv[2, at])
+        pooled = (psend[0, at] + precv[0, at]) + (precv[1, at] + precv[2, at])
         grad = up[at]
         mixed = cross(pooled, 0) + bias[...]
         back[0, at] = grad * mixed + cross(grad * pooled, 2) + grad
-        for j in (2, 1):
+        for j in (2, 3, 1) if h else (2, 1):
             zcp[j, h] = send(block(0, 0, h), block(0, j, h), bz_sem.at[j - 1, h], line[j])
         forward(0, h)
         crossed_ref[at] = pooled * mixed + pooled
 
     def along(j, h):
         zcp[j, h].wait_recv()
-        if j == 2:
+        if j == 2 and h == 0:
             zcp[3, h] = send(block(0, 2, h), block(0, 3, h), bz_sem.at[2, h], line[1])
         forward(j, h)
 
@@ -203,59 +207,69 @@
 
     process(0)
     idy.wait()
-    count(2, 0)
+    counts(2)
+    along(1, 0)
+    diagonal(0, 0)
     process(1)
     stores = [pltpu.make_async_copy(crossed_ref, crossed_out, store_sem.at[0])]
     stores[0].start()
-    along(1, 0)
     along(2, 0)
-    diagonal(0, 0)
-    count(2, 1)
+    diagonal(1, 0)
+    idd.wait()
+    counts(3)
     along(3, 0)
     along(1, 1)
-    diagonal(1, 0)
+    diagonal(0, 1)
     along(2, 1)
-    diagonal(0, 1)
-    idd.wait()
-    count(3, 0)
     diagonal(2, 0)
     along(3, 1)
     diagonal(1, 1)
     diagonal(3, 0)
-    count(3, 1)
     diagonal(2, 1)
     diagonal(3, 1)
 
-    def product(r, start=0, size=2 * rows):
+    def product(r, q):
         bh, bl = split(back[r])
-        c = ct[r, start : start + size]
-        g[r, start : start + size] = dot(c, bh) + dot(c, bl)
-
-    product(0)
-    product(1)
-    product(2)
+        at = pl.ds(pl.multiple_of(q * CHUNK, CHUNK), CHUNK)
+        c = jnp.concatenate([ct[r, 0, at], ct[r, 1, at]], axis=1)
+        g[r, at] = dot(c, bh) + dot(c, bl)
+        return at
+
+    def early(i, carry):
+        product(i // (2 * per_block), i % (2 * per_block))
+        return carry
+
+    lax.fori_loop(0, (PLANE - 1) * 2 * per_block, early, 0)
     for cp in dcp.values():
         cp.wait_recv()
 
-    def finish(start, size):
-        product(3, start, size)
-        at = slice(start, start + size)
+    def swap(i):
+        return pltpu.make_async_remote_copy(
+            src_ref=g.at[0, pl.ds(rows + i * CHUNK, CHUNK)],
+            dst_ref=grecv.at[pl.ds(i * CHUNK, CHUNK)],
+            send_sem=g_sem.at[i, 0], recv_sem=g_sem.at[i, 1],
+            device_id=mate, device_id_type=MESH,
+        )
+
+    def late(i, carry):
+        q = (i + per_block) % (2 * per_block)
+        at = product(3, q)
         g[0, at] = (g[0, at] + g[1, at]) + (g[2, at] + g[3, at])
 
-    piece = rows // 2
-    gcp = []
-    for i in range(2):
-        finish(rows + i * piece, piece)
-        gcp.append(
-            send(g.at[0, pl.ds(rows + i * piece, piece)], grecv.at[pl.ds(i * piece, piece)], g_sem.at[i], mate)
-        )
-    finish(0, rows)
+        @pl.when(i < per_block)
+        def _():
+            swap(i).start()
+
+        return carry
+
+    lax.fori_loop(0, 2 * per_block, late, 0)
+    piece = CHUNK
     acc_col = jnp.transpose(jnp.broadcast_to(accum[...], (8, rows)))[:, 0:1]
     for d in (zcp, xcp, ycp, dcp):
         for cp in d.values():
             cp.wait_send()
-    for i in range(2):
-        gcp[i].wait()
+    for i in range(per_block):
+        swap(i).wait()
         at = slice(i * piece, (i + 1) * piece)
         total = g[0, at] + grecv[at]
         mean = jnp.sum(total * total, axis=1, keepdims=True) * (1.0 / total.shape[1])
@@ -265,7 +279,7 @@
         stores.append(pltpu.make_async_copy(newt_ref.at[part], newt_out.at[part], store_sem.at[1 + i]))
         stores[-1].start()
         newa_ref[:, at] = jnp.transpose(jnp.broadcast_to(fresh, (piece, 128)))[0:1]
-    stores.append(pltpu.make_async_copy(newa_ref, newa_out, store_sem.at[3]))
+    stores.append(pltpu.make_async_copy(newa_ref, newa_out, store_sem.at[1 + per_block]))
     stores[-1].start()
     for cp in stores:
         cp.wait()
@@ -307,8 +321,8 @@
             pltpu.VMEM((2 * rows, width), BF16),
             pltpu.VMEM((2 * rows, width), BF16),
             pltpu.VMEM((PLANE, LINE, tall, 128), jnp.int32),
-            pltpu.VMEM((PLANE, 2 * rows, LINE * each), BF16),
-            pltpu.VMEM((LINE - 1, each, width), F32),
+            pltpu.VMEM((PLANE, 2, 2 * rows, 2 * each), BF16),
+            pltpu.VMEM((LINE, each, width), F32),
             pltpu.VMEM((LINE - 1, each, width), F32),
             pltpu.VMEM((PLANE, LINE * each, width), F32),
             pltpu.VMEM((PLANE, 2 * rows, width), F32),
@@ -323,7 +337,7 @@
             pltpu.VMEM((rows, width), F32),
             pltpu.VMEM((1, rows), F32),
             dma((6,)),
-            dma((4,)),
+            dma((2 + rows // CHUNK,)),
             dma((2,)),
             dma((3, 2)),
             dma((3, 2)),
@@ -331,7 +345,7 @@
             dma((3, 2, 2)),
             dma((2, LINE, 2, 2)),
             dma((LINE, 2, 2)),
-            dma((2, 2)),
+            dma((rows // CHUNK, 2)),
         ],
         compiler_params=pltpu.CompilerParams(
             collective_id=0, has_side_effects=True, vmem_limit_bytes=GRANT

time: 37.6 us -> 37.4 us (level)
  no operation moved by 1% of the time
where the time goes in v1:
time: 37.4 us; the launch traced here: 37.2 us
  Pallas kernels  36.6 us (98%)
  between operations  0.64 us (2%)
    pallas_call x1, Pallas kernels, fused_body(): pl.pallas_call(lambda *refs: kernel(bag, *refs), out_shape=shapes, in_spe...  34.7 us
    pallas_call x1, Pallas kernels, fused_body(): pl.pallas_call(hand_out, out_shape=shapes, in_specs=[hbm] * 3, out_specs=...  1.82 us

profile of v1, /device:TPU:0, one launch (start us, length us, event | category | flops | bytes accessed | tf_op | source)
XLA Modules:
  0.0 37.2 jit_solution(10006107547098076603)
XLA Ops:
  0.6 34.7 %shard_map.85 = (f32[64,256]{1,0:T(8,128)}, f32[512,256]{1,0:T(8,128)}, f32[1,512]{1,0:T(1,128)}) custom-call(s32[20,64]{1,0:T(8,128)} %bitcast.4, f32[512,256]{1,0:T(8,128)} %refs_1_.1, f32[1,512]{1,0:T(1,128)} %bitcast.5, f32[256,256]{1,0:T(8,128)} %refs_3_.1, f32[1,256]{1,0:T(1,128)} %bitcast.6, f32[64,256]{1,0:T(8,128)} %refs_5_.1), custom_call_target="tpu_custom_call" | custom-call | tf_op jit(solution)/shard_map/pallas_call | solution.py:314
  35.4 1.8 %shard_map.86 = (f32[64,256]{1,0:T(8,128)}, f32[512,256]{1,0:T(8,128)}, f32[1,512]{1,0:T(1,128)}) custom-call(f32[64,256]{1,0:T(8,128)} %get-tuple-element.9.a, f32[512,256]{1,0:T(8,128)} %get-tuple-element.10.b, f32[1,512]{1,0:T(1,128)} %get-tuple-element.11.c), custom_call_target="tpu_custom_call" | custom-call | tf_op jit(solution)/shard_map/pallas_call | solution.py:354

commit v2 on v1

--- a/solution.py
+++ b/solution.py
@@ -10,6 +10,7 @@
 MESH = pl.DeviceIdType.MESH
 PLANE = 4
 LINE = 4
+SLAB = 128
 GRANT = 63 * 1024 * 1024
 CHUNK = 256
 
@@ -77,8 +78,11 @@
     pl.semaphore_wait(barrier, 6)
 
     idz = {j: send(ids.at[0, 0], ids.at[0, j], idz_sem.at[j - 1], line[j]) for j in (2, 3, 1)}
-    tcp = send(table_hbm, tab.at[1], tab_sem, mate)
     table_load.wait()
+    tcp = []
+    for i in range(rows // SLAB):
+        part = pl.ds(i * SLAB, SLAB)
+        tcp.append(send(tab.at[0, part], tab.at[1, part], tab_sem.at[i], mate))
     hi, lo = split(tab[0])
     thi[0:rows] = hi
     tlo[0:rows] = lo
@@ -121,7 +125,7 @@
                 acc = jnp.where(widen(local[j : j + 1]) == row16, widen(times[j : j + 1]), acc)
             at = pl.ds(pl.multiple_of(q * CHUNK, CHUNK), CHUNK)
             ct[r, p, at] = acc
-            return carry if use is None else use(acc, at, carry)
+            return carry if use is None else use(acc, at, carry, q)
 
         return lax.fori_loop(0, 2 * per_block, step, start)
 
@@ -138,21 +142,27 @@
         part = pl.ds(h * half, half)
         pcp[j, h] = send(psend.at[j, part], precv.at[j - 1, part], p_sem.at[j - 1, h], line[j])
 
-    def add_part(acc, at, total):
+    def first_part(acc, at, total, q):
+        @pl.when(q == per_block)
+        def _():
+            for cp in tcp:
+                cp.wait()
+            hi, lo = split(tab[1])
+            thi[rows : 2 * rows] = hi
+            tlo[rows : 2 * rows] = lo
+
+        return add_part(acc, at, total, q)
+
+    def add_part(acc, at, total, q):
         return total + dot(acc, thi[at], ((0,), (0,))) + dot(acc, tlo[at], ((0,), (0,)))
 
     for p in (1, 0):
         for j in ((2, 3) if p else (1,)):
             idz[j].wait()
-        if p:
-            tcp.wait()
-            hi, lo = split(tab[1])
-            thi[rows : 2 * rows] = hi
-            tlo[rows : 2 * rows] = lo
-        else:
+        if not p:
             idx = send(ids.at[0], ids.at[1], idp_sem.at[0], xn)
             idy = send(ids.at[0], ids.at[2], idp_sem.at[1], yn)
-        part = count(0, p, add_part, jnp.zeros((128, tab.shape[2]), F32))
+        part = count(0, p, first_part if p else add_part, jnp.zeros((128, tab.shape[2]), F32))
         psend[2 * p] = part[0:each]
         psend[2 * p + 1] = part[each : 2 * each]
         for j in (2 * p, 2 * p + 1):
@@ -245,8 +255,8 @@
 
     def swap(i):
         return pltpu.make_async_remote_copy(
-            src_ref=g.at[0, pl.ds(rows + i * CHUNK, CHUNK)],
-            dst_ref=grecv.at[pl.ds(i * CHUNK, CHUNK)],
+            src_ref=g.at[0, pl.ds(rows + i * SLAB, SLAB)],
+            dst_ref=grecv.at[pl.ds(i * SLAB, SLAB)],
             send_sem=g_sem.at[i, 0], recv_sem=g_sem.at[i, 1],
             device_id=mate, device_id_type=MESH,
         )
@@ -258,7 +268,8 @@
 
         @pl.when(i < per_block)
         def _():
-            swap(i).start()
+            for k in range(CHUNK // SLAB):
+                swap(i * (CHUNK // SLAB) + k).start()
 
         return carry
 
@@ -269,7 +280,8 @@
         for cp in d.values():
             cp.wait_send()
     for i in range(per_block):
-        swap(i).wait()
+        for k in range(CHUNK // SLAB):
+            swap(i * (CHUNK // SLAB) + k).wait()
         at = slice(i * piece, (i + 1) * piece)
         total = g[0, at] + grecv[at]
         mean = jnp.sum(total * total, axis=1, keepdims=True) * (1.0 / total.shape[1])
@@ -338,14 +350,14 @@
             pltpu.VMEM((1, rows), F32),
             dma((6,)),
             dma((2 + rows // CHUNK,)),
-            dma((2,)),
+            dma((rows // SLAB, 2)),
             dma((3, 2)),
             dma((3, 2)),
             dma((3, 2, 2)),
             dma((3, 2, 2)),
             dma((2, LINE, 2, 2)),
             dma((LINE, 2, 2)),
-            dma((rows // CHUNK, 2)),
+            dma((rows // SLAB, 2)),
         ],
         compiler_params=pltpu.CompilerParams(
             collective_id=0, has_side_effects=True, vmem_limit_bytes=GRANT

time: 37.4 us -> 37.7 us (level)
  no operation moved by 1% of the time
where the time goes in v2:
time: 37.7 us; the launch traced here: 37.5 us
  Pallas kernels  36.8 us (98%)
  between operations  0.64 us (2%)
    pallas_call x1, Pallas kernels, fused_body(): pl.pallas_call(lambda *refs: kernel(bag, *refs), out_shape=shapes, in_spe...  35 us
    pallas_call x1, Pallas kernels, fused_body(): pl.pallas_call(hand_out, out_shape=shapes, in_specs=[hbm] * 3, out_specs=...  1.82 us

profile of v2, /device:TPU:0, one launch (start us, length us, event | category | flops | bytes accessed | tf_op | source)
XLA Modules:
  0.0 37.5 jit_solution(13726874834219278770)
XLA Ops:
  0.6 35.0 %shard_map.85 = (f32[64,256]{1,0:T(8,128)}, f32[512,256]{1,0:T(8,128)}, f32[1,512]{1,0:T(1,128)}) custom-call(s32[20,64]{1,0:T(8,128)} %bitcast.4, f32[512,256]{1,0:T(8,128)} %refs_1_.1, f32[1,512]{1,0:T(1,128)} %bitcast.5, f32[256,256]{1,0:T(8,128)} %refs_3_.1, f32[1,256]{1,0:T(1,128)} %bitcast.6, f32[64,256]{1,0:T(8,128)} %refs_5_.1), custom_call_target="tpu_custom_call" | custom-call | tf_op jit(solution)/shard_map/pallas_call | solution.py:326
  35.6 1.8 %shard_map.86 = (f32[64,256]{1,0:T(8,128)}, f32[512,256]{1,0:T(8,128)}, f32[1,512]{1,0:T(1,128)}) custom-call(f32[64,256]{1,0:T(8,128)} %get-tuple-element.9.a, f32[512,256]{1,0:T(8,128)} %get-tuple-element.10.b, f32[1,512]{1,0:T(1,128)} %get-tuple-element.11.c), custom_call_target="tpu_custom_call" | custom-call | tf_op jit(solution)/shard_map/pallas_call | solution.py:366

commit v3 on v2

--- a/solution.py
+++ b/solution.py
@@ -232,11 +232,14 @@
     diagonal(0, 1)
     along(2, 1)
     diagonal(2, 0)
+    dcp[0, 1].wait_recv()
+    for j in (2, 3, 1):
+        dcp[j, 1] = send(block(3, 0, 1), block(3, j, 1), bd_sem.at[j, 1], line[j])
     along(3, 1)
-    diagonal(1, 1)
     diagonal(3, 0)
-    diagonal(2, 1)
-    diagonal(3, 1)
+    for j in (1, 2, 3):
+        xcp[j, 1].wait_recv()
+        ycp[j, 1].wait_recv()
 
     def product(r, q):
         bh, bl = split(back[r])
@@ -250,8 +253,9 @@
         return carry
 
     lax.fori_loop(0, (PLANE - 1) * 2 * per_block, early, 0)
-    for cp in dcp.values():
-        cp.wait_recv()
+    for at, cp in dcp.items():
+        if at != (0, 1):
+            cp.wait_recv()
 
     def swap(i):
         return pltpu.make_async_remote_copy(

time: 37.7 us -> 39.2 us (1.040)
  Pallas kernels: 36.8 us -> 38.3 us
    pallas_call x1, Pallas kernels: 35 us -> 36.5 us  [fused_body(): pl.pallas_call(lambda *refs: kernel(bag, *refs), out_shape=shapes, in_spe...]
where the time goes in v3:
time: 39.2 us; the launch traced here: 38.9 us
  Pallas kernels  38.3 us (98%)
  between operations  0.64 us (2%)
    pallas_call x1, Pallas kernels, fused_body(): pl.pallas_call(lambda *refs: kernel(bag, *refs), out_shape=shapes, in_spe...  36.5 us
    pallas_call x1, Pallas kernels, fused_body(): pl.pallas_call(hand_out, out_shape=shapes, in_specs=[hbm] * 3, out_specs=...  1.82 us

profile of v3, /device:TPU:0, one launch (start us, length us, event | category | flops | bytes accessed | tf_op | source)
XLA Modules:
  0.0 38.9 jit_solution(13216422851172112093)
XLA Ops:
  0.6 36.5 %shard_map.85 = (f32[64,256]{1,0:T(8,128)}, f32[512,256]{1,0:T(8,128)}, f32[1,512]{1,0:T(1,128)}) custom-call(s32[20,64]{1,0:T(8,128)} %bitcast.4, f32[512,256]{1,0:T(8,128)} %refs_1_.1, f32[1,512]{1,0:T(1,128)} %bitcast.5, f32[256,256]{1,0:T(8,128)} %refs_3_.1, f32[1,256]{1,0:T(1,128)} %bitcast.6, f32[64,256]{1,0:T(8,128)} %refs_5_.1), custom_call_target="tpu_custom_call" | custom-call | tf_op jit(solution)/shard_map/pallas_call | solution.py:330
  37.1 1.8 %shard_map.86 = (f32[64,256]{1,0:T(8,128)}, f32[512,256]{1,0:T(8,128)}, f32[1,512]{1,0:T(1,128)}) custom-call(f32[64,256]{1,0:T(8,128)} %get-tuple-element.9.a, f32[512,256]{1,0:T(8,128)} %get-tuple-element.10.b, f32[1,512]{1,0:T(1,128)} %get-tuple-element.11.c), custom_call_target="tpu_custom_call" | custom-call | tf_op jit(solution)/shard_map/pallas_call | solution.py:370

commit v4 on v1

--- a/solution.py
+++ b/solution.py
@@ -39,6 +39,7 @@
     mate = (rep, shard + 1 - 2 * core)
     xn = (rep + 1 - 2 * (rep % 2), shard)
     yn = ((rep + 2) % 4, shard)
+    dn = (PLANE - 1 - rep, shard)
     line = {
         1: (rep, (z + 1 - 2 * (z % 2)) * 2 + core),
         2: (rep, ((z + 2) % LINE) * 2 + core),
@@ -54,7 +55,7 @@
         return cp
 
     barrier = pltpu.get_barrier_semaphore()
-    for to in (mate, xn, yn, line[1], line[2], line[3]):
+    for to in (mate, xn, yn, dn, line[1], line[2], line[3]):
         pl.semaphore_signal(barrier, inc=1, device_id=to, device_id_type=MESH)
 
     def load(src, dst, i):
@@ -74,7 +75,7 @@
     raw = ids_raw[...]
     ids[0, 0] = jnp.full(ids.shape[2:], -1, jnp.int32)
     ids[0, 0, 0:bag] = jnp.concatenate([raw, raw], axis=1)
-    pl.semaphore_wait(barrier, 6)
+    pl.semaphore_wait(barrier, 7)
 
     idz = {j: send(ids.at[0, 0], ids.at[0, j], idz_sem.at[j - 1], line[j]) for j in (2, 3, 1)}
     tcp = send(table_hbm, tab.at[1], tab_sem, mate)
@@ -196,6 +197,8 @@
         if j == 2 and h == 0:
             zcp[3, h] = send(block(0, 2, h), block(0, 3, h), bz_sem.at[2, h], line[1])
         forward(j, h)
+        if h and j > 1:
+            dcp[j, h] = send(block(0, j, h), block(3, j, h), bd_sem.at[j, h], dn)
 
     def diagonal(j, h):
         xcp[j, h].wait_recv()
@@ -225,8 +228,6 @@
     along(3, 1)
     diagonal(1, 1)
     diagonal(3, 0)
-    diagonal(2, 1)
-    diagonal(3, 1)
 
     def product(r, q):
         bh, bl = split(back[r])
@@ -235,11 +236,18 @@
         g[r, at] = dot(c, bh) + dot(c, bl)
         return at
 
-    def early(i, carry):
-        product(i // (2 * per_block), i % (2 * per_block))
-        return carry
-
-    lax.fori_loop(0, (PLANE - 1) * 2 * per_block, early, 0)
+    def whole(r):
+        bh, bl = split(back[r])
+        c = jnp.concatenate([ct[r, 0], ct[r, 1]], axis=1)
+        g[r] = dot(c, bh) + dot(c, bl)
+
+    whole(0)
+    for j in (2, 3):
+        xcp[j, 1].wait_recv()
+    whole(1)
+    for j in (2, 3):
+        ycp[j, 1].wait_recv()
+    whole(2)
     for cp in dcp.values():
         cp.wait_recv()
 

time: 37.4 us -> 36.2 us (0.968)
  Pallas kernels: 36.6 us -> 35.3 us
    pallas_call x1, Pallas kernels: 34.7 us -> 33.5 us  [fused_body(): pl.pallas_call(lambda *refs: kernel(bag, *refs), out_shape=shapes, in_spe...]
where the time goes in v4:
time: 36.2 us; the launch traced here: 35.9 us
  Pallas kernels  35.3 us (98%)
  between operations  0.64 us (2%)
    pallas_call x1, Pallas kernels, fused_body(): pl.pallas_call(lambda *refs: kernel(bag, *refs), out_shape=shapes, in_spe...  33.5 us
    pallas_call x1, Pallas kernels, fused_body(): pl.pallas_call(hand_out, out_shape=shapes, in_specs=[hbm] * 3, out_specs=...  1.82 us

profile of v4, /device:TPU:0, one launch (start us, length us, event | category | flops | bytes accessed | tf_op | source)
XLA Modules:
  0.0 35.9 jit_solution(12032680382689537545)
XLA Ops:
  0.6 33.5 %shard_map.85 = (f32[64,256]{1,0:T(8,128)}, f32[512,256]{1,0:T(8,128)}, f32[1,512]{1,0:T(1,128)}) custom-call(s32[20,64]{1,0:T(8,128)} %bitcast.4, f32[512,256]{1,0:T(8,128)} %refs_1_.1, f32[1,512]{1,0:T(1,128)} %bitcast.5, f32[256,256]{1,0:T(8,128)} %refs_3_.1, f32[1,256]{1,0:T(1,128)} %bitcast.6, f32[64,256]{1,0:T(8,128)} %refs_5_.1), custom_call_target="tpu_custom_call" | custom-call | tf_op jit(solution)/shard_map/pallas_call | solution.py:322
  34.1 1.8 %shard_map.86 = (f32[64,256]{1,0:T(8,128)}, f32[512,256]{1,0:T(8,128)}, f32[1,512]{1,0:T(1,128)}) custom-call(f32[64,256]{1,0:T(8,128)} %get-tuple-element.9.a, f32[512,256]{1,0:T(8,128)} %get-tuple-element.10.b, f32[1,512]{1,0:T(1,128)} %get-tuple-element.11.c), custom_call_target="tpu_custom_call" | custom-call | tf_op jit(solution)/shard_map/pallas_call | solution.py:362
